TPU v7x, 32 devices: a whole 2x2x4 slice. The times are simulated.
32 devices in a mesh: feat: 4 (over y, x), node: 8 (over z, core).
Axes of the slice: x: 2, y: 2, z: 4, core: 2. Of those that a mesh axis runs over, the one named last changes fastest.
Arguments:
- features: bfloat16 [8192, 1024], P('node', 'feat'), may hold values from -6 to 6
- tile_values: bfloat16 [8, 24, 128, 128], P('node'), may hold values from 0.0009994507 to 1
- tile_coords: int32 [8, 24, 2], P('node'), may hold values from 0 to 7, as said below
- tile_count: int32 [8], P('node'), may hold values from 8 to 24, as said below
- halo_index: int32 [8, 8, 4], P('node'), may hold values from 0 to 1023
- halo_weight: bfloat16 [8, 1024, 32], P('node'), may hold values from 0.0009994507 to 1
- first_self: bfloat16 [1024, 256], P('feat'), may hold values from -0.1875 to 0.1875
- first_neighbour: bfloat16 [1024, 256], P('feat'), may hold values from -3 to 3
- second_self: bfloat16 [256, 256], replicated, may hold values from -0.375 to 0.375
- second_neighbour: bfloat16 [256, 256], replicated, may hold values from -1.5 to 1.5
- upstream: bfloat16 [8192, 256], P(('node', 'feat')), may hold values from -6 to 6
- seed_flags: int32 [8192], P(('node', 'feat')), may hold values 0 or 1
Outputs:
- embedding: bfloat16 [8192, 256], P(('node', 'feat'))
- grad_first_self: float32 [1024, 256], P('feat')
- grad_first_neighbour: float32 [1024, 256], P('feat')
- grad_second_self: float32 [256, 256], replicated
- grad_second_neighbour: float32 [256, 256], replicated
Inputs may be any that keep to these rules, and one draw needn't show every extreme that they name: `tile_coords`: the 24 slots of a partition name distinct pairs (destination block, source block) of its 8 blocks; only slots below tile_count are live. `tile_count`: some partition has all 24 slots live in every draw.
All inputs are finite; a program needn't handle non-finite values. No bound on the sum of `seed_flags` on one device may be relied on, other than what follows from the above.
Results may differ from a plain program's by a relative error of at most 0.015.
Values may be sent and summed in bfloat16 or wider, within the bound.
A program may use at most 64 MiB of HBM per device.

v0:
```python
import math

import jax
import jax.numpy as jnp
from jax import lax
from jax.sharding import PartitionSpec as P

HIGHEST_PRECISION = lax.Precision.HIGHEST


def silu_slope(value):
    sigm = jax.nn.sigmoid(value)
    return sigm * (1.0 + value * (1.0 - sigm))


def tile_sum(values, read_ids, write_ids, live_slots, source, targets):
    tile_side = values.shape[1]
    blocks = source.shape[0] // tile_side
    block_ids = jnp.arange(blocks, dtype=jnp.int32)
    read_pick = (read_ids[:, None] == block_ids[None, :]).astype(jnp.bfloat16)
    write_pick = ((write_ids[:, None] == targets[None, :]) & live_slots[:, None]).astype(
        jnp.float32
    )
    stacked = source.reshape(blocks, tile_side, source.shape[1])
    chosen = jnp.einsum(
        "tb,bnw->tnw", read_pick, stacked, preferred_element_type=jnp.float32
    ).astype(jnp.bfloat16)
    products = jnp.einsum("tij,tjw->tiw", values, chosen, preferred_element_type=jnp.float32)
    running = jnp.einsum("tb,tiw->biw", write_pick, products, precision=HIGHEST_PRECISION)
    row_sums = jnp.einsum(
        "tb,ti->bi",
        write_pick,
        jnp.sum(values, axis=2, dtype=jnp.float32),
        precision=HIGHEST_PRECISION,
    )
    return (running.reshape(-1, source.shape[1]), row_sums.reshape(-1))


def tile_matrix(values, coords, live_slots, row_ids, col_ids):
    source_pick = (coords[:, 1][:, None] == col_ids[None, :]).astype(jnp.bfloat16)
    target_pick = ((coords[:, 0][:, None] == row_ids[None, :]) & live_slots[:, None]).astype(
        jnp.bfloat16
    )
    paired = jnp.einsum(
        "tb,tc->tbc", target_pick, source_pick, preferred_element_type=jnp.float32
    ).astype(jnp.bfloat16)
    dense_tiles = jnp.einsum("tbc,tij->bicj", paired, values, preferred_element_type=jnp.float32)
    tile_side = values.shape[1]
    return dense_tiles.astype(jnp.bfloat16).reshape(
        row_ids.shape[0] * tile_side, col_ids.shape[0] * tile_side
    )


def on_device(
    features,
    tile_values,
    tile_coords,
    tile_count,
    halo_index,
    halo_weight,
    first_self,
    first_neighbour,
    second_self,
    second_neighbour,
    upstream,
    seed_flags,
):
    part_rows, feat_width = features.shape
    values = tile_values[0]
    coords = tile_coords[0]
    tile_side = values.shape[1]
    blocks = part_rows // tile_side
    own_rows = upstream.shape[0]
    own_blocks = own_rows // tile_side
    live_slots = jnp.arange(values.shape[0], dtype=jnp.int32) < tile_count[0]
    all_blocks = jnp.arange(blocks, dtype=jnp.int32)
    feat_group = lax.axis_index("feat")
    own_start = feat_group * own_rows
    own_ids = feat_group * own_blocks + jnp.arange(own_blocks, dtype=jnp.int32)
    contract = (((0,), (0,)), ((), ()))
    against = (((1,), (1,)), ((), ()))
    outgoing = jnp.take(features, halo_index[0], axis=0)
    incoming = lax.all_to_all(outgoing, "node", split_axis=0, concat_axis=0, tiled=True)
    boundary = incoming.reshape(-1, feat_width)
    numerator, tile_degree = tile_sum(
        values, coords[:, 1], coords[:, 0], live_slots, features, all_blocks
    )
    weights = halo_weight[0]
    halo_part = jnp.dot(weights, boundary, preferred_element_type=jnp.float32)
    degree_one = 1.0 + tile_degree + jnp.sum(weights, axis=1, dtype=jnp.float32)
    aggregated = ((numerator + halo_part) / degree_one[:, None]).astype(jnp.bfloat16)
    adjacency = tile_matrix(values, coords, live_slots, own_ids, all_blocks)
    degree_two = 1.0 + jnp.sum(adjacency, axis=1, dtype=jnp.float32)
    partial_sums = jnp.dot(features, first_self, preferred_element_type=jnp.float32) + jnp.dot(
        aggregated, first_neighbour, preferred_element_type=jnp.float32
    )
    preact_all = lax.psum(partial_sums.astype(jnp.bfloat16), "feat").astype(jnp.float32)
    hidden_all = jax.nn.silu(preact_all).astype(jnp.bfloat16)
    hidden_own = lax.dynamic_slice_in_dim(hidden_all, own_start, own_rows, 0)
    layer_sum = jnp.dot(adjacency, hidden_all, preferred_element_type=jnp.float32)
    neighbour_mean = (layer_sum / degree_two[:, None]).astype(jnp.bfloat16)
    embedding = (
        jnp.dot(hidden_own, second_self, preferred_element_type=jnp.float32)
        + jnp.dot(neighbour_mean, second_neighbour, preferred_element_type=jnp.float32)
    ).astype(jnp.bfloat16)
    cot_scale = 1.0 / math.sqrt(part_rows * lax.axis_size("node"))
    cotangent = (
        upstream.astype(jnp.float32) * seed_flags[:, None].astype(jnp.float32) * cot_scale
    ).astype(jnp.bfloat16)
    grad_two_self = lax.dot_general(
        hidden_own, cotangent, contract, preferred_element_type=jnp.float32
    )
    grad_two_neigh = lax.dot_general(
        neighbour_mean, cotangent, contract, preferred_element_type=jnp.float32
    )
    scaled_grad = (
        lax.dot_general(cotangent, second_neighbour, against, preferred_element_type=jnp.float32)
        / degree_two[:, None]
    ).astype(jnp.bfloat16)
    own_term = lax.dot_general(cotangent, second_self, against, preferred_element_type=jnp.float32)
    spread_back = lax.dot_general(
        adjacency, scaled_grad, contract, preferred_element_type=jnp.float32
    )
    own_part = lax.dynamic_slice_in_dim(spread_back, own_start, own_rows, 0) + own_term
    grad_partial = lax.dynamic_update_slice_in_dim(spread_back, own_part, own_start, 0)
    grad_all, grad_two_self, grad_two_neigh = (
        lax.psum(grad_partial.astype(jnp.bfloat16), "feat").astype(jnp.float32),
        lax.psum(grad_two_self.astype(jnp.bfloat16), "feat").astype(jnp.float32),
        lax.psum(grad_two_neigh.astype(jnp.bfloat16), "feat").astype(jnp.float32),
    )
    grad_preact = (grad_all * silu_slope(preact_all)).astype(jnp.bfloat16)
    grad_one_self = lax.dot_general(
        features, grad_preact, contract, preferred_element_type=jnp.float32
    )
    grad_one_neigh = lax.dot_general(
        aggregated, grad_preact, contract, preferred_element_type=jnp.float32
    )
    summed = lax.psum((grad_one_self, grad_one_neigh, grad_two_self, grad_two_neigh), "node")
    return (embedding, summed[0], summed[1], summed[2], summed[3])


def solution(mesh):
    in_specs = (
        P("node", "feat"),
        P("node", None, None, None),
        P("node", None, None),
        P("node"),
        P("node", None, None),
        P("node", None, None),
        P("feat", None),
        P("feat", None),
        P(),
        P(),
        P(("node", "feat"), None),
        P(("node", "feat")),
    )
    out_specs = (P(("node", "feat"), None), P("feat", None), P("feat", None), P(), P())
    return jax.shard_map(
        on_device, mesh=mesh, in_specs=in_specs, out_specs=out_specs, check_vma=False
    )
```

profile of v0, /device:TPU:0, one launch (start us, length us, event | category | flops | bytes accessed | tf_op | source)
XLA Modules:
  0.0 206.9 jit_solution(11096730104257751170)
XLA Ops:
  7.2 0.0 copy-start
  7.2 0.0 copy-start.1
  7.2 0.8 compare_select_fusion
  8.0 0.7 compare_and_fusion
  8.7 0.1 copy.23
  8.7 0.1 reshape.92
  8.8 0.0 copy-done
  8.8 0.6 gather_fusion
  9.5 0.1 copy.22
  9.6 0.7 broadcast_select_fusion
  10.3 6.3 %all-to-all-start = ((bf16[8,4,256]{2,1,0:T(4,128)(2,1)}), bf16[8,4,256]{2,1,0:T(4,128)(2,1)S(1)}, u32[]{:S(2)}, u32[]{:S(2)}) async-start(bf16[8,4,256]{2,1,0:T(4,128)(2,1)} %broadcast_select_fusion), calls=%async_computation | async-start | bytes 32768 | tf_op jit(solution)/shard_map/all_to_all | solution.py:83
  16.6 0.0 all-reduce.8.cloned.1.call-start
  16.7 0.8 slice_bitcast_fusion.1
  17.4 0.6 fusion.26
  18.0 0.0 copy-done.1
  18.1 0.3 convert_reduce_fusion
  18.3 2.3 %fusion.2 = f32[24,256,128]{2,1,0:T(8,128)} fusion(bf16[24,128,256]{2,0,1:T(8,128)(2,1)S(1)} %fusion.26, bf16[1,24,128,128]{3,2,1,0:T(8,128)(2,1)S(1)} %copy-done.1), kind=kOutput, calls=%fused_computation.4 | convolution fusion | flops 201326592 | bytes 5505024 | tf_op jit(solution)/shard_map/tij,tjw->tiw/dot_general | solution.py:28
  20.6 3.6 %copy.29 = f32[24,256,128]{1,0,2:T(8,128)} copy(f32[24,256,128]{2,1,0:T(8,128)} %fusion.2) | data formatting | bytes 6291456 | tf_op jit(solution)/shard_map/tij,tjw->tiw/dot_general | solution.py:28
  24.9 0.0 copy-done.11
  24.9 0.0 copy-done.10
  24.9 0.3 fusion.54
  25.2 3.1 %fusion = f32[8,128,256]{2,0,1:T(8,128)S(1)} fusion(f32[24,256,128]{1,0,2:T(8,128)} %copy.29, s32[24]{0:T(128)S(1)} %get-tuple-element.22, pred[24]{0:T(512)(128)(4,1)S(1)} %iota_compare_fusion.2), kind=kOutput, calls=%fused_computation.1 | convolution fusion | flops 75497856 | bytes 4194424 | tf_op jit(solution)/shard_map/tb,tiw->biw/dot_general | solution.py:29
  28.3 0.1 and_convert_fusion
  28.4 1.9 convert_reduce_fusion.1
  30.2 0.1 fusion.13
  30.4 0.3 copy.21
  30.7 1.3 copy.24
  32.0 0.0 all-to-all-done
  32.0 0.0 copy-start.5
  32.1 1.6 fusion.5
  33.6 0.0 copy-done.5
  33.7 0.0 copy-start.12
  33.7 0.0 copy-start.3
  33.7 0.0 copy-start.6
  33.7 0.0 copy-start.9
  33.7 1.1 fusion.6
  34.8 0.0 all-reduce.8.cloned.1.call-update
  34.9 0.0 all-reduce.12.cloned.1.call-start
  34.9 0.0 copy-done.12
  35.0 0.0 copy-done.3
  35.0 0.0 copy-done.6
  35.0 0.6 fusion.11
  35.6 0.2 copy-done.4
  35.7 0.2 fusion.7
  36.0 0.9 convert_element_type.95
  36.9 44.9 %all-reduce.8.cloned.1.call-done = bf16[1024,256]{1,0:T(8,128)(2,1)} async-done(((bf16[1024,256]{1,0:T(8,128)(2,1)}), bf16[1024,256]{1,0:T(8,128)(2,1)}) %all-reduce.8.cloned.1.call-update) | async-done | bytes 524304 | tf_op jit(solution)/shard_map/psum | solution.py:97
  81.8 1.3 fusion.17
  83.1 0.3 fusion.10
  83.5 0.0 copy-start.2
  83.5 0.9 convolution_convert_fusion.2
  84.4 0.9 convolution_convert_fusion.1
  85.3 0.0 all-reduce.12.cloned.1.call-update
  85.4 0.0 all-reduce.10.cloned.1.call-start
  85.4 0.2 fusion.32
  85.6 49.3 %all-reduce.12.cloned.1.call-done = (bf16[256,256]{1,0:T(8,128)(2,1)}, bf16[256,256]{1,0:T(8,128)(2,1)}, bf16[1024,256]{1,0:T(8,128)(2,1)}) async-done(((bf16[256,256]{1,0:T(8,128)(2,1)}, bf16[256,256]{1,0:T(8,128)(2,1)}, bf16[1024,256]{1,0:T(8,128)(2,1)}), (bf16[256,256]{1,0:T(8,128)(2,1)}, bf16[256,256]{1,0:T(8,128)(2,1)}, bf16[1024,256]{1,0:T(8,128)(2,1)})) %all-reduce.12.cloned.1.call-update) | async-done | bytes 786448 | tf_op jit(solution)/shard_map/psum | solution.py:128
  134.9 1.5 fusion.21
  136.4 1.0 fusion.55
  137.4 1.0 convolution_bitcast_fusion.1
  138.5 0.0 all-reduce.10.cloned.1.call-update
  138.5 0.8 fusion.8
  139.3 37.0 %all-reduce.13 = (f32[256,256]{1,0:T(8,128)}, f32[256,256]{1,0:T(8,128)}) all-reduce(bf16[256,256]{1,0:T(8,128)(2,1)S(1)} %copy-done.7, bf16[256,256]{1,0:T(8,128)(2,1)S(1)} %copy-done.8), channel_id=1, replica_groups=mesh['feat'=4,'node'=8] {'node'}, use_global_device_ids=true, to_apply=%region_8.9 | all-reduce | flops 131072 | bytes 786432 | tf_op jit(solution)/shard_map/psum | solution.py:138
  176.3 20.6 %all-reduce.10.cloned.1.call-done = (f32[256,256]{0,1:T(8,128)}, f32[256,256]{1,0:T(8,128)}) async-done(((f32[256,256]{0,1:T(8,128)}, f32[256,256]{1,0:T(8,128)}), (f32[256,256]{0,1:T(8,128)}, f32[256,256]{1,0:T(8,128)})) %all-reduce.10.cloned.1.call-update) | async-done | bytes 524304 | tf_op jit(solution)/shard_map/psum | solution.py:138
  196.9 1.8 copy.26
  198.7 1.7 copy.62
  (18 shorter events, 0.1 us)
Async XLA Ops:
  7.2 1.7 copy-start
  7.2 10.9 %copy-start.1 = (bf16[1,24,128,128]{3,2,1,0:T(8,128)(2,1)S(1)}, bf16[1,24,128,128]{3,2,1,0:T(8,128)(2,1)}, u32[]{:S(2)}) copy-start(bf16[1,24,128,128]{3,2,1,0:T(8,128)(2,1)} %param.13) | copy-start | bytes 2359300
  10.3 21.8 %all-to-all-start = ((bf16[8,4,256]{2,1,0:T(4,128)(2,1)}), bf16[8,4,256]{2,1,0:T(4,128)(2,1)S(1)}, u32[]{:S(2)}, u32[]{:S(2)}) async-start(bf16[8,4,256]{2,1,0:T(4,128)(2,1)} %broadcast_select_fusion), calls=%async_computation | async-start | bytes 32768 | tf_op jit(solution)/shard_map/all_to_all | solution.py:83
  16.6 65.2 %all-reduce.8.cloned.1.call-start = ((), (), s32[]{:S(2)}) async-start(), calls=%async_computation.1 | async-start | bytes 1048576 | tf_op jit(solution)/shard_map/psum | solution.py:97
  20.6 4.3 %copy-start.11 = (bf16[1,1024,32]{1,2,0:T(8,128)(2,1)S(1)}, bf16[1,1024,32]{1,2,0:T(8,128)(2,1)}, u32[]{:S(2)}) copy-start(bf16[1,1024,32]{1,2,0:T(8,128)(2,1)} %param.17) | copy-start | bytes 196612
  20.6 4.3 %copy-start.10 = (bf16[256,256]{1,0:T(8,128)(2,1)S(1)}, bf16[256,256]{1,0:T(8,128)(2,1)}, u32[]{:S(2)}) copy-start(bf16[256,256]{1,0:T(8,128)(2,1)} %param.18) | copy-start | bytes 393220
  32.0 1.6 copy-start.5
  33.7 1.3 copy-start.12
  33.7 1.3 copy-start.3
  33.7 1.3 copy-start.6
  33.7 1.3 copy-start.9
  34.8 0.9 copy-start.4
  34.9 100.1 %all-reduce.12.cloned.1.call-start = ((), (), s32[]{:S(2)}) async-start(), calls=%async_computation.3 | async-start | bytes 1572864 | tf_op jit(solution)/shard_map/psum | solution.py:128
  83.5 51.5 %copy-start.2 = (bf16[1024,256]{1,0:T(8,128)(2,1)S(1)}, bf16[1024,256]{1,0:T(8,128)(2,1)}, u32[]{:S(2)}) copy-start(bf16[1024,256]{1,0:T(8,128)(2,1)} %all-reduce.8.cloned.1.call-done) | copy-start | bytes 1572868
  85.4 111.5 %all-reduce.10.cloned.1.call-start = ((), (), s32[]{:S(2)}) async-start(), calls=%async_computation.2 | async-start | bytes 1048576 | tf_op jit(solution)/shard_map/psum | solution.py:138
  137.4 1.9 copy-start.7
  137.4 1.9 copy-start.8
Sparse Core Ops, SparseCore 0:
  35.0 46.7 all-reduce.7
  85.7 49.2 all-reduce.11
  138.6 58.2 all-reduce.9
where the time goes:
time: 207 us
  waiting for transfers between devices  115 us (56%)
  blocking collectives  37 us (18%)
  matrix products  17 us (8%)
  between operations  14.7 us (7%)
  local copies, waits for them, and re-layouts  10.6 us (5%)
  starting transfers between devices  6.45 us (3%)
  other arithmetic  6.27 us (3%)
    psum x1, waiting for transfers between devices, on_device(): lax.psum(grad_two_self.astype(jnp.bfloat16), 'feat').astype(jnp.float32)  49.3 us
    psum x1, waiting for transfers between devices, on_device(): lax.psum(partial_sums.astype(jnp.bfloat16), 'feat').astype(jnp.float32)  44.9 us
    psum x1, blocking collectives, on_device(): lax.psum((grad_one_self, grad_one_neigh, grad_two_self, grad_two_neigh),...  37 us
    psum x1, waiting for transfers between devices, on_device(): lax.psum((grad_one_self, grad_one_neigh, grad_two_self, grad_two_neigh),...  20.6 us
    all_to_all x1, starting transfers between devices, on_device(): lax.all_to_all(outgoing, 'node', split_axis=0, concat_axis=0, tiled=True)  6.33 us
  transfers between devices with their start and end apart: 4, of which 3 were waited for; matrix products, arithmetic and copies ran while one was open for 8% of the time, Pallas kernels for 0%

commit v1 on v0

--- a/solution.py
+++ b/solution.py
@@ -1,8 +1,11 @@
+import functools
 import math
 
 import jax
 import jax.numpy as jnp
 from jax import lax
+from jax.experimental import pallas as pl
+from jax.experimental.pallas import tpu as pltpu
 from jax.sharding import PartitionSpec as P
 
 HIGHEST_PRECISION = lax.Precision.HIGHEST
@@ -139,7 +142,447 @@
     return (embedding, summed[0], summed[1], summed[2], summed[3])
 
 
+FUSED_NODES = 8
+HALO_ROWS = 16
+MESH_ID = pl.DeviceIdType.MESH
+
+
+def nn(a, b):
+    return jnp.dot(a, b, preferred_element_type=jnp.float32)
+
+
+def nt(a, b):
+    return lax.dot_general(a, b, (((1,), (1,)), ((), ())), preferred_element_type=jnp.float32)
+
+
+def step_kernel(
+    groups, nodes,
+    feats, tvals, coords, count, hidx, hweight, w1s, w1n, w2s, w2n, upstream, flags,
+    emb_o, g1s_o, g1n_o, g2s_o, g2n_o,
+    x_v, tiles, tiles_t, hw_v, w1s_v, w1n_v, w2s_v, w2n_v, up_v, slot_v, slot_s,
+    adj, adj_t, numer, deg, agg, x_t, agg_t, cot, cot_t, scaled, grad_h,
+    hsend, hrecv, psend, precv, pre, hid, mean, gpre,
+    s1, r1s, comb1, r1z, g1fin, s2, r2s, comb2, r2z, g2fin,
+    ld_sem, halo_ss, halo_rs, cot_ss, cot_rs, rs_ss, rs_rs, ag_ss, ag_rs,
+    sib_ss, sib_rs, z_ss, z_rs, zg_ss, zg_rs, fg_ss, fg_rs, fw_ss, fw_rs,
+):
+    f = lax.axis_index("feat")
+    n = lax.axis_index("node")
+    zs = nodes // 2
+    z, c = n // 2, n % 2
+    rows, width = x_v.shape
+    slots = tiles.shape[0] - 1
+    side = tiles.shape[1]
+    blocks = rows // side
+    own = up_v.shape[0]
+    units = w1s_v.shape[1]
+    outs = w2s_v.shape[1]
+    cap = hidx.shape[2]
+
+    def local(src, dst, i):
+        copy = pltpu.make_async_copy(src, dst, ld_sem.at[i])
+        copy.start()
+        return copy
+
+    def remote(src, dst, ss, rs, where):
+        return pltpu.make_async_remote_copy(
+            src_ref=src, dst_ref=dst, send_sem=ss, recv_sem=rs,
+            device_id=where, device_id_type=MESH_ID,
+        )
+
+    def feat_at(d):
+        return lax.rem(f + d, groups)
+
+    def feat_id(d):
+        return {"feat": feat_at(d)}
+
+    def z_at(d):
+        return lax.rem(z + d, zs)
+
+    def z_id(d):
+        return {"node": z_at(d) * 2 + c}
+
+    sib_id = {"node": z * 2 + (1 - c)}
+
+    def own_rows(p):
+        return pl.ds(pl.multiple_of(p * own, own), own)
+
+    ld_up = local(upstream, up_v, 0)
+    ld_x = local(feats, x_v, 1)
+    ld_t = local(tvals.at[0], tiles.at[pl.ds(0, slots)], 2)
+    ld_hw = local(hweight.at[0], hw_v, 3)
+    ld_1s = local(w1s, w1s_v, 4)
+    ld_1n = local(w1n, w1n_v, 5)
+    ld_2s = local(w2s, w2s_v, 6)
+    ld_2n = local(w2n, w2n_v, 7)
+
+    barrier = pltpu.get_barrier_semaphore()
+    for d in range(1, groups):
+        pl.semaphore_signal(barrier, inc=1, device_id=feat_id(d), device_id_type=MESH_ID)
+    for d in range(1, nodes):
+        pl.semaphore_signal(
+            barrier, inc=1, device_id={"node": lax.rem(n + d, nodes)}, device_id_type=MESH_ID
+        )
+
+    pairs = coords[0]
+    key = pairs[:, 0:1] * blocks + pairs[:, 1:2]
+    slot_id = lax.broadcasted_iota(jnp.int32, (slots, 128), 0)
+    pair_id = lax.broadcasted_iota(jnp.int32, (slots, 128), 1)
+    named = (key == pair_id) & (slot_id < count[0])
+    slot_v[...] = jnp.broadcast_to(
+        jnp.min(jnp.where(named, slot_id, slots), axis=0, keepdims=True), slot_v.shape
+    )
+    ld_slot = local(slot_v, slot_s, 8)
+    tiles[slots] = jnp.zeros((side, side), jnp.bfloat16)
+    tiles_t[slots] = jnp.zeros((side, side), jnp.bfloat16)
+
+    scale = 1.0 / math.sqrt(rows * nodes)
+    r_id = lax.broadcasted_iota(jnp.int32, (own, own), 0)
+    c_id = lax.broadcasted_iota(jnp.int32, (own, own), 1)
+    picked = jnp.where((r_id == c_id) & (flags[...] != 0), 1.0, 0.0).astype(jnp.bfloat16)
+    ld_up.wait()
+    cot[own_rows(f), :] = (nn(picked, up_v[...]) * scale).astype(jnp.bfloat16)
+    row_id = lax.broadcasted_iota(jnp.int32, (HALO_ROWS, rows), 0)
+    col_id = lax.broadcasted_iota(jnp.int32, (HALO_ROWS, rows), 1)
+    parts = []
+    for q in range(nodes):
+        want = jnp.full((HALO_ROWS, rows), -1, jnp.int32)
+        for k in range(cap):
+            want = jnp.where(row_id == k, hidx[0, q, k], want)
+        parts.append(jnp.where(want == col_id, 1.0, 0.0).astype(jnp.bfloat16))
+    picks = jnp.concatenate(parts, axis=0)
+    ld_x.wait()
+    hsend[...] = nn(picks, x_v[...]).astype(jnp.bfloat16).reshape(hsend.shape)
+    hrecv[n] = hsend[n]
+
+    pl.semaphore_wait(barrier, groups - 1 + nodes - 1)
+    halo_copies = []
+    for d in range(1, nodes):
+        q = lax.rem(n + d, nodes)
+        copy = remote(hsend.at[q], hrecv.at[n], halo_ss.at[d], halo_rs.at[d], {"node": q})
+        copy.start()
+        halo_copies.append(copy)
+    cot_copies = []
+    for d in range(1, groups):
+        mine = cot.at[own_rows(f)]
+        copy = remote(mine, mine, cot_ss.at[d], cot_rs.at[d], feat_id(d))
+        copy.start()
+        cot_copies.append(copy)
+
+    ld_t.wait()
+    ld_slot.wait()
+    for r in range(blocks):
+        for s in range(blocks):
+            adj[r * side:(r + 1) * side, s * side:(s + 1) * side] = tiles[
+                slot_s[0, r * blocks + s]
+            ]
+    ones_a = jnp.ones((rows, 128), jnp.bfloat16)
+
+    @pl.loop(0, groups)
+    def _(d):
+        at = own_rows(d)
+        tile_rows = adj[at, :]
+        numer[at, :] = nn(tile_rows, x_v[...])
+        deg[at, :] = 1.0 + nn(tile_rows, ones_a)
+
+    ld_hw.wait()
+    ld_1s.wait()
+    ld_1n.wait()
+    for d, copy in enumerate(halo_copies):
+        copy.wait_recv()
+    halo = nodes * cap
+    e_row = lax.broadcasted_iota(jnp.int32, (halo, nodes * HALO_ROWS), 0)
+    e_col = lax.broadcasted_iota(jnp.int32, (halo, nodes * HALO_ROWS), 1)
+    spread = (e_row // cap) * HALO_ROWS + e_row % cap
+    unpad = jnp.where(spread == e_col, 1.0, 0.0).astype(jnp.bfloat16)
+    bound = nn(unpad, hrecv[...].reshape(nodes * HALO_ROWS, width)).astype(jnp.bfloat16)
+    ones_h = jnp.ones((halo, 128), jnp.bfloat16)
+
+    def first_layer(p):
+        at = own_rows(p)
+        weights = hw_v[at, :]
+        inverse = 1.0 / (deg[at, :] + nn(weights, ones_h))
+        inverse = jnp.concatenate([inverse] * (width // 128), axis=1)
+        mixed = ((numer[at, :] + nn(weights, bound)) * inverse).astype(jnp.bfloat16)
+        agg[at, :] = mixed
+        return nn(x_v[at, :], w1s_v[...]) + nn(mixed, w1n_v[...])
+
+    rs_copies = []
+    for d in range(1, groups):
+        psend[d] = first_layer(feat_at(d)).astype(jnp.bfloat16)
+        copy = remote(psend.at[d], precv.at[d], rs_ss.at[d], rs_rs.at[d], feat_id(d))
+        copy.start()
+        rs_copies.append(copy)
+    total = first_layer(f)
+
+    for k in range(groups):
+        at = slice(k * own, (k + 1) * own)
+        x_t[:, at] = x_v[at, :].T
+        agg_t[:, at] = agg[at, :].T
+    for copy in rs_copies:
+        copy.wait_recv()
+    for d in range(1, groups):
+        total = total + precv[d].astype(jnp.float32)
+    pre[own_rows(f), :] = total.astype(jnp.bfloat16)
+    ag_copies = []
+    for d in range(1, groups):
+        mine = pre.at[own_rows(f)]
+        copy = remote(mine, mine, ag_ss.at[d], ag_rs.at[d], feat_id(d))
+        copy.start()
+        ag_copies.append(copy)
+
+    for t in range(slots):
+        tiles_t[t] = tiles[t].T
+    for r in range(blocks):
+        for s in range(blocks):
+            adj_t[s * side:(s + 1) * side, r * side:(r + 1) * side] = tiles_t[
+                slot_s[0, r * blocks + s]
+            ]
+    ld_2s.wait()
+    ld_2n.wait()
+    for copy in cot_copies:
+        copy.wait_recv()
+    for k in range(groups):
+        at = slice(k * own, (k + 1) * own)
+        cot_t[:, at] = cot[at, :].T
+
+    @pl.loop(0, groups)
+    def _(d):
+        at = own_rows(d)
+        inverse = 1.0 / deg[at, :]
+        deg[at, :] = inverse
+        inverse = jnp.concatenate([inverse] * (units // 128), axis=1)
+        scaled[at, :] = (nt(cot[at, :], w2n_v[...]) * inverse).astype(jnp.bfloat16)
+
+    @pl.loop(0, groups)
+    def _(d):
+        at = own_rows(d)
+        grad_h[at, :] = nt(cot[at, :], w2s_v[...]) + nn(adj_t[at, :], scaled[...])
+
+    def activate(p):
+        at = own_rows(p)
+        value = pre[at, :].astype(jnp.float32)
+        sigm = jax.nn.sigmoid(value)
+        hid[at, :] = (value * sigm).astype(jnp.bfloat16)
+        slope = sigm * (1.0 + value * (1.0 - sigm))
+        gpre[at, :] = (grad_h[at, :] * slope).astype(jnp.bfloat16)
+
+    activate(f)
+    for d in range(groups - 1, 0, -1):
+        ag_copies[d - 1].wait_recv()
+        activate(feat_at(groups - d))
+
+    piece = width // nodes
+    for k, lhs in enumerate((x_t, agg_t)):
+        grad = nn(lhs[...], gpre[...])
+        for q in range(nodes):
+            s1[q % 2, q // 2, k * piece:(k + 1) * piece, :] = grad[
+                q * piece:(q + 1) * piece
+            ].astype(jnp.bfloat16)
+    sib1 = remote(s1.at[1 - c], r1s, sib_ss.at[0], sib_rs.at[0], sib_id)
+    sib1.start()
+
+    @pl.loop(0, groups)
+    def _(d):
+        at = own_rows(d)
+        inverse = jnp.concatenate([deg[at, :]] * (units // 128), axis=1)
+        mean[at, :] = (nn(adj[at, :], hid[...]) * inverse).astype(jnp.bfloat16)
+
+    share = outs // groups
+    bit = share // nodes
+    cot_rows = cot_t[pl.ds(pl.multiple_of(f * share, share), share), :]
+    both = (nn(cot_rows, hid[...]), nn(cot_rows, mean[...]))
+    for q in range(nodes):
+        s2[q % 2, q // 2] = jnp.concatenate(
+            [grad[q * bit:(q + 1) * bit] for grad in both], axis=0
+        ).astype(jnp.bfloat16)
+    sib2 = remote(s2.at[1 - c], r2s, sib_ss.at[1], sib_rs.at[1], sib_id)
+    sib2.start()
+
+    z_copies = []
+    for i, (sib, mine, theirs, comb, dest) in enumerate(
+        ((sib1, s1, r1s, comb1, r1z), (sib2, s2, r2s, comb2, r2z))
+    ):
+        sib.wait_recv()
+        comb[...] = (mine[c].astype(jnp.float32) + theirs[...].astype(jnp.float32)).astype(
+            jnp.bfloat16
+        )
+        batch = []
+        for d in range(1, zs):
+            copy = remote(
+                comb.at[z_at(d)], dest.at[d], z_ss.at[i, d], z_rs.at[i, d], z_id(d)
+            )
+            copy.start()
+            batch.append(copy)
+        z_copies.append(batch)
+
+    at = own_rows(f)
+    emb_o[...] = (nn(hid[at, :], w2s_v[...]) + nn(mean[at, :], w2n_v[...])).astype(jnp.bfloat16)
+
+    gathers = []
+    for i, (comb, dest, final) in enumerate(
+        ((comb1, r1z, g1fin.at[c]), (comb2, r2z, g2fin.at[f, c]))
+    ):
+        total = comb[z].astype(jnp.float32)
+        for d in range(1, zs):
+            z_copies[i][d - 1].wait_recv()
+            total = total + dest[d].astype(jnp.float32)
+        if i == 0:
+            g1fin[c, z] = total.astype(jnp.bfloat16)
+        else:
+            g2fin[f, c, z] = total.astype(jnp.bfloat16)
+        batch = []
+        for d in range(1, zs):
+            copy = remote(
+                final.at[z], final.at[z], zg_ss.at[i, d], zg_rs.at[i, d], z_id(d)
+            )
+            copy.start()
+            batch.append(copy)
+        gathers.append(batch)
+
+    def forward(ref, i):
+        copy = remote(ref, ref, fw_ss.at[i], fw_rs.at[i], sib_id)
+        copy.start()
+        return copy
+
+    forwards = [forward(g1fin.at[c, z], 0)]
+    for copy in gathers[1]:
+        copy.wait_recv()
+    feat_copies = []
+    for d in range(1, groups):
+        mine = g2fin.at[f, c]
+        copy = remote(mine, mine, fg_ss.at[d], fg_rs.at[d], feat_id(d))
+        copy.start()
+        feat_copies.append(copy)
+    forwards.append(forward(g2fin.at[f, c], 1))
+    for d in range(1, zs):
+        gathers[0][d - 1].wait_recv()
+        forwards.append(forward(g1fin.at[c, z_at(zs - d)], 1 + d))
+    for d in range(1, groups):
+        feat_copies[d - 1].wait_recv()
+        forwards.append(forward(g2fin.at[feat_at(groups - d), c], zs + d))
+    for copy in forwards:
+        copy.wait_recv()
+
+    for q in range(nodes):
+        at = slice(q * piece, (q + 1) * piece)
+        g1s_o[at, :] = g1fin[q % 2, q // 2, :piece, :].astype(jnp.float32)
+        g1n_o[at, :] = g1fin[q % 2, q // 2, piece:, :].astype(jnp.float32)
+    for k, out in enumerate((g2s_o, g2n_o)):
+        out[...] = jnp.concatenate(
+            [
+                g2fin[g, q % 2, q // 2].astype(jnp.float32)[k * bit:(k + 1) * bit]
+                for g in range(groups)
+                for q in range(nodes)
+            ],
+            axis=0,
+        ).T
+
+    for copy in halo_copies + cot_copies + rs_copies + ag_copies + [sib1, sib2]:
+        copy.wait_send()
+    for batch in z_copies + gathers:
+        for copy in batch:
+            copy.wait_send()
+    for copy in feat_copies + forwards:
+        copy.wait_send()
+
+
+def fused_step(
+    groups, nodes, features, tile_values, tile_coords, tile_count, halo_index, halo_weight,
+    first_self, first_neighbour, second_self, second_neighbour, upstream, seed_flags,
+):
+    rows, width = features.shape
+    slots, side = tile_values.shape[1], tile_values.shape[2]
+    halo = halo_weight.shape[2]
+    own, outs = upstream.shape
+    units = first_self.shape[1]
+    zs = nodes // 2
+    piece = 2 * width // nodes
+    bit = 2 * outs // groups // nodes
+    b16, f32 = jnp.bfloat16, jnp.float32
+    vmem, anywhere, smem = (
+        pl.BlockSpec(memory_space=kind) for kind in (pltpu.VMEM, pl.ANY, pltpu.SMEM)
+    )
+    dma = pltpu.SemaphoreType.DMA
+    scratch = [
+        pltpu.VMEM((rows, width), b16),
+        pltpu.VMEM((slots + 1, side, side), b16),
+        pltpu.VMEM((slots + 1, side, side), b16),
+        pltpu.VMEM((rows, halo), b16),
+        pltpu.VMEM((width, units), b16),
+        pltpu.VMEM((width, units), b16),
+        pltpu.VMEM((units, outs), b16),
+        pltpu.VMEM((units, outs), b16),
+        pltpu.VMEM((own, outs), b16),
+        pltpu.VMEM((8, 128), jnp.int32),
+        pltpu.SMEM((8, 128), jnp.int32),
+        pltpu.VMEM((rows, rows), b16),
+        pltpu.VMEM((rows, rows), b16),
+        pltpu.VMEM((rows, width), f32),
+        pltpu.VMEM((rows, 128), f32),
+        pltpu.VMEM((rows, width), b16),
+        pltpu.VMEM((width, rows), b16),
+        pltpu.VMEM((width, rows), b16),
+        pltpu.VMEM((rows, outs), b16),
+        pltpu.VMEM((outs, rows), b16),
+        pltpu.VMEM((rows, units), b16),
+        pltpu.VMEM((rows, units), f32),
+        pltpu.VMEM((nodes, HALO_ROWS, width), b16),
+        pltpu.VMEM((nodes, HALO_ROWS, width), b16),
+        pltpu.VMEM((groups, own, units), b16),
+        pltpu.VMEM((groups, own, units), b16),
+        pltpu.VMEM((rows, units), b16),
+        pltpu.VMEM((rows, units), b16),
+        pltpu.VMEM((rows, units), b16),
+        pltpu.VMEM((rows, units), b16),
+        pltpu.VMEM((2, zs, piece, units), b16),
+        pltpu.VMEM((zs, piece, units), b16),
+        pltpu.VMEM((zs, piece, units), b16),
+        pltpu.VMEM((zs, piece, units), b16),
+        pltpu.VMEM((2, zs, piece, units), b16),
+        pltpu.VMEM((2, zs, bit, units), b16),
+        pltpu.VMEM((zs, bit, units), b16),
+        pltpu.VMEM((zs, bit, units), b16),
+        pltpu.VMEM((zs, bit, units), b16),
+        pltpu.VMEM((groups, 2, zs, bit, units), b16),
+        dma((9,)),
+        dma((nodes,)), dma((nodes,)),
+        dma((groups,)), dma((groups,)),
+        dma((groups,)), dma((groups,)),
+        dma((groups,)), dma((groups,)),
+        dma((2,)), dma((2,)),
+        dma((2, zs)), dma((2, zs)),
+        dma((2, zs)), dma((2, zs)),
+        dma((groups,)), dma((groups,)),
+        dma((zs + groups,)), dma((zs + groups,)),
+    ]
+    return pl.pallas_call(
+        functools.partial(step_kernel, groups, nodes),
+        out_shape=(
+            jax.ShapeDtypeStruct((own, outs), b16),
+            jax.ShapeDtypeStruct((width, units), f32),
+            jax.ShapeDtypeStruct((width, units), f32),
+            jax.ShapeDtypeStruct((units, outs), f32),
+            jax.ShapeDtypeStruct((units, outs), f32),
+        ),
+        in_specs=[
+            anywhere, anywhere, vmem, smem, smem, anywhere, anywhere, anywhere, anywhere,
+            anywhere, anywhere, vmem,
+        ],
+        out_specs=(vmem,) * 5,
+        scratch_shapes=scratch,
+        compiler_params=pltpu.CompilerParams(
+            collective_id=0, has_side_effects=True, vmem_limit_bytes=40 * 1024 * 1024
+        ),
+    )(
+        features, tile_values, tile_coords, tile_count, halo_index, halo_weight, first_self,
+        first_neighbour, second_self, second_neighbour, upstream, seed_flags.reshape(1, own),
+    )
+
+
 def solution(mesh):
+    groups, nodes = mesh.shape["feat"], mesh.shape["node"]
+    step = functools.partial(fused_step, groups, nodes) if nodes <= FUSED_NODES else on_device
     in_specs = (
         P("node", "feat"),
         P("node", None, None, None),
@@ -156,5 +599,5 @@
     )
     out_specs = (P(("node", "feat"), None), P("feat", None), P("feat", None), P(), P())
     return jax.shard_map(
-        on_device, mesh=mesh, in_specs=in_specs, out_specs=out_specs, check_vma=False
-    )
+        step, mesh=mesh, in_specs=in_specs, out_specs=out_specs, check_vma=False
+    )

time: 207 us -> 57.7 us (0.28)
  waiting for transfers between devices: 115 us -> 0 us
  Pallas kernels: 0 us -> 45.7 us
  blocking collectives: 37 us -> 0 us
  matrix products: 17 us -> 0 us
  between operations: 14.7 us -> 1.36 us
  starting transfers between devices: 6.45 us -> 0 us
  other arithmetic: 6.27 us -> 0 us
    psum x3 -> x0, waiting for transfers between devices: 115 us -> none  [the longest x1 49.3 us: on_device(): lax.psum(grad_two_self.astype(jnp.bfloat16), 'feat').astype(jnp.float32)]
    pallas_call x0 -> x1, Pallas kernels: none -> 45.7 us  [fused_step(): pl.pallas_call(functools.partial(step_kernel, groups, nodes), out_shape=(...]
    psum x1 -> x0, blocking collectives: 37 us -> none  [on_device(): lax.psum((grad_one_self, grad_one_neigh, grad_two_self, grad_two_neigh),...]
    dot_general x17 -> x0, matrix products: 17 us -> none  [the longest x1 3.07 us: tile_sum(): jnp.einsum('tb,tiw->biw', write_pick, products, precision=HIGHEST_PRECISION)]
    unnamed x28, local copies, waits for them, and re-layouts: 3.7 us -> 10.2 us
    all_to_all x1 -> x0, starting transfers between devices: 6.33 us -> none  [on_device(): lax.all_to_all(outgoing, 'node', split_axis=0, concat_axis=0, tiled=True)]
    dot_general x2 -> x0, local copies, waits for them, and re-layouts: 3.96 us -> none  [the longest x1 3.61 us: tile_sum(): jnp.einsum('tij,tjw->tiw', values, chosen, preferred_element_type=jnp.flo...]
    convert_element_type x4 -> x0, other arithmetic: 3.71 us -> none  [the longest x1 1.47 us: on_device(): grad_preact = (grad_all * silu_slope(preact_all)).astype(jnp.bfloat16)]
  transfers between devices with their start and end apart: 4 -> 0, of which waited for: 3 -> 0; matrix products, arithmetic and copies ran while one was open for 8% -> 0% of each run, Pallas kernels for 0% -> 0%
where the time goes in v1:
time: 57.7 us; the launch traced here: 57.2 us
  Pallas kernels  45.7 us (79%)
  local copies, waits for them, and re-layouts  10.2 us (18%)
  between operations  1.36 us (2%)
    pallas_call x1, Pallas kernels, fused_step(): pl.pallas_call(functools.partial(step_kernel, groups, nodes), out_shape=(...  45.7 us
    unnamed x28, local copies, waits for them, and re-layouts  10.2 us

profile of v1, /device:TPU:0, one launch (start us, length us, event | category | flops | bytes accessed | tf_op | source)
XLA Modules:
  0.0 57.2 jit_solution(10618817968639324273)
XLA Ops:
  0.6 0.0 copy-start.8
  1.3 0.0 copy-done.8
  1.3 0.0 copy-start.9
  1.3 0.1 copy.18.hidx
  1.4 0.6 %copy-done.9 = s32[1,24,2]{1,2,0:T(2,128)S(1)} copy-done((s32[1,24,2]{1,2,0:T(2,128)S(1)}, s32[1,24,2]{1,2,0:T(2,128)}, u32[]{:S(2)}) %copy-start.9) | copy-done | bytes 216
  2.0 0.1 copy.17.coords
  2.1 0.0 copy-start.2
  2.1 0.0 copy-start.3
  2.1 0.0 copy-start.7
  2.1 1.0 %copy.19.hweight = bf16[1,1024,32]{2,1,0:T(8,128)(2,1)S(1)} copy(bf16[1,1024,32]{1,2,0:T(8,128)(2,1)} %param.17) | data formatting | bytes 131072 | tf_op args[5]
  3.1 0.0 copy-done.2
  3.2 0.0 copy-done.3
  3.2 0.0 copy-done.7
  3.2 0.0 copy-start
  3.2 1.1 %copy-done = bf16[1,24,128,128]{3,2,1,0:T(8,128)(2,1)S(1)} copy-done((bf16[1,24,128,128]{3,2,1,0:T(8,128)(2,1)S(1)}, bf16[1,24,128,128]{3,2,1,0:T(8,128)(2,1)}, u32[]{:S(2)}) %copy-start) | copy-done | bytes 786456
  4.3 0.0 copy-start.1
  4.3 1.0 %copy-done.1 = bf16[1024,256]{1,0:T(8,128)(2,1)S(1)} copy-done((bf16[1024,256]{1,0:T(8,128)(2,1)S(1)}, bf16[1024,256]{1,0:T(8,128)(2,1)}, u32[]{:S(2)}) %copy-start.1) | copy-done | bytes 524312
  5.3 0.0 copy-start.4
  5.4 0.9 %copy-done.4 = bf16[256,256]{1,0:T(8,128)(2,1)S(1)} copy-done((bf16[256,256]{1,0:T(8,128)(2,1)S(1)}, bf16[256,256]{1,0:T(8,128)(2,1)}, u32[]{:S(2)}) %copy-start.4) | copy-done | bytes 131096
  6.3 0.0 copy-start.5
  6.3 0.9 %copy-done.5 = bf16[256,256]{1,0:T(8,128)(2,1)S(1)} copy-done((bf16[256,256]{1,0:T(8,128)(2,1)S(1)}, bf16[256,256]{1,0:T(8,128)(2,1)}, u32[]{:S(2)}) %copy-start.5) | copy-done | bytes 131096
  7.2 0.0 copy-start.6
  7.2 0.9 %copy-done.6 = bf16[256,256]{1,0:T(8,128)(2,1)S(1)} copy-done((bf16[256,256]{1,0:T(8,128)(2,1)S(1)}, bf16[256,256]{1,0:T(8,128)(2,1)}, u32[]{:S(2)}) %copy-start.6) | copy-done | bytes 131096
  8.1 45.7 %shard_map.155 = (bf16[256,256]{1,0:T(8,128)(2,1)S(1)}, f32[256,256]{1,0:T(8,128)S(1)}, f32[256,256]{1,0:T(8,128)S(1)}, f32[256,256]{1,0:T(8,128)S(1)}, f32[256,256]{1,0:T(8,128)S(1)}) custom-call(bf16[1024,256]{1,0:T(8,128)(2,1)S(1)} %copy-done.1, bf16[1,24,128,128]{3,2,1,0:T(8,128)(2,1)S(1)} %copy-done, s32[1,24,2]{2,1,0:T(8,128)S(1)} %copy.17.coords, ...), custom_call_target="tpu_custom_call" | custom-call | tf_op jit(solution)/shard_map/pallas_call | solution.py:559
  53.8 0.7 %copy.26 = bf16[256,256]{1,0:T(8,128)(2,1)} copy(bf16[256,256]{1,0:T(8,128)(2,1)S(1)} %get-tuple-element.10) | data formatting | bytes 262144
  54.4 0.7 %copy.27 = f32[256,256]{1,0:T(8,128)} copy(f32[256,256]{1,0:T(8,128)S(1)} %get-tuple-element.11) | data formatting | bytes 524288
  55.1 0.7 %copy.28 = f32[256,256]{1,0:T(8,128)} copy(f32[256,256]{1,0:T(8,128)S(1)} %get-tuple-element.12) | data formatting | bytes 524288
  55.8 0.7 %copy.29 = f32[256,256]{1,0:T(8,128)} copy(f32[256,256]{1,0:T(8,128)S(1)} %get-tuple-element.13) | data formatting | bytes 524288
  56.5 0.7 %copy.30 = f32[256,256]{1,0:T(8,128)} copy(f32[256,256]{1,0:T(8,128)S(1)} %get-tuple-element.14) | data formatting | bytes 524288
Async XLA Ops:
  0.6 0.7 %copy-start.8 = (s32[1,8,4]{1,2,0:T(4,128)S(1)}, s32[1,8,4]{1,2,0:T(4,128)}, u32[]{:S(2)}) copy-start(s32[1,8,4]{1,2,0:T(4,128)} %param.16) | copy-start | bytes 388
  1.3 0.7 %copy-start.9 = (s32[1,24,2]{1,2,0:T(2,128)S(1)}, s32[1,24,2]{1,2,0:T(2,128)}, u32[]{:S(2)}) copy-start(s32[1,24,2]{1,2,0:T(2,128)} %param.14) | copy-start | bytes 580
  2.1 1.1 %copy-start.2 = (bf16[256,256]{1,0:T(8,128)(2,1)S(1)}, bf16[256,256]{1,0:T(8,128)(2,1)}, u32[]{:S(2)}) copy-start(bf16[256,256]{1,0:T(8,128)(2,1)} %w1s.1) | copy-start | bytes 393220
  2.1 1.1 %copy-start.3 = (bf16[256,256]{1,0:T(8,128)(2,1)S(1)}, bf16[256,256]{1,0:T(8,128)(2,1)}, u32[]{:S(2)}) copy-start(bf16[256,256]{1,0:T(8,128)(2,1)} %w1n.1) | copy-start | bytes 393220
  2.1 1.1 %copy-start.7 = (s32[256]{0:T(256)S(1)}, s32[256]{0:T(256)}, u32[]{:S(2)}) copy-start(s32[256]{0:T(256)} %param.23) | copy-start | bytes 3076
  3.2 1.1 %copy-start = (bf16[1,24,128,128]{3,2,1,0:T(8,128)(2,1)S(1)}, bf16[1,24,128,128]{3,2,1,0:T(8,128)(2,1)}, u32[]{:S(2)}) copy-start(bf16[1,24,128,128]{3,2,1,0:T(8,128)(2,1)} %tvals.1) | copy-start | bytes 2359300
  4.3 1.0 %copy-start.1 = (bf16[1024,256]{1,0:T(8,128)(2,1)S(1)}, bf16[1024,256]{1,0:T(8,128)(2,1)}, u32[]{:S(2)}) copy-start(bf16[1024,256]{1,0:T(8,128)(2,1)} %feats.1) | copy-start | bytes 1572868
  5.3 0.9 %copy-start.4 = (bf16[256,256]{1,0:T(8,128)(2,1)S(1)}, bf16[256,256]{1,0:T(8,128)(2,1)}, u32[]{:S(2)}) copy-start(bf16[256,256]{1,0:T(8,128)(2,1)} %w2s.1) | copy-start | bytes 393220
  6.3 0.9 %copy-start.5 = (bf16[256,256]{1,0:T(8,128)(2,1)S(1)}, bf16[256,256]{1,0:T(8,128)(2,1)}, u32[]{:S(2)}) copy-start(bf16[256,256]{1,0:T(8,128)(2,1)} %w2n.1) | copy-start | bytes 393220
  7.2 0.9 %copy-start.6 = (bf16[256,256]{1,0:T(8,128)(2,1)S(1)}, bf16[256,256]{1,0:T(8,128)(2,1)}, u32[]{:S(2)}) copy-start(bf16[256,256]{1,0:T(8,128)(2,1)} %upstream.1) | copy-start | bytes 393220

commit v2 on v1

--- a/solution.py
+++ b/solution.py
@@ -158,8 +158,8 @@
 def step_kernel(
     groups, nodes,
     feats, tvals, coords, count, hidx, hweight, w1s, w1n, w2s, w2n, upstream, flags,
-    emb_o, g1s_o, g1n_o, g2s_o, g2n_o,
-    x_v, tiles, tiles_t, hw_v, w1s_v, w1n_v, w2s_v, w2n_v, up_v, slot_v, slot_s,
+    emb_o, g1_o, g2_o,
+    x_v, tiles, tiles_t, coords_v, flags_v, hidx_s, hw_t, hw_v, w1s_v, w1n_v, w2s_v, w2n_v, up_v, slot_v, slot_s,
     adj, adj_t, numer, deg, agg, x_t, agg_t, cot, cot_t, scaled, grad_h,
     hsend, hrecv, psend, precv, pre, hid, mean, gpre,
     s1, r1s, comb1, r1z, g1fin, s2, r2s, comb2, r2z, g2fin,
@@ -177,7 +177,7 @@
     own = up_v.shape[0]
     units = w1s_v.shape[1]
     outs = w2s_v.shape[1]
-    cap = hidx.shape[2]
+    cap = hidx.shape[1]
 
     def local(src, dst, i):
         copy = pltpu.make_async_copy(src, dst, ld_sem.at[i])
@@ -207,10 +207,13 @@
     def own_rows(p):
         return pl.ds(pl.multiple_of(p * own, own), own)
 
+    ld_flags = local(flags, flags_v, 9)
     ld_up = local(upstream, up_v, 0)
+    ld_hidx = local(hidx.at[0], hidx_s, 10)
+    ld_coords = local(coords.at[0], coords_v, 11)
     ld_x = local(feats, x_v, 1)
     ld_t = local(tvals.at[0], tiles.at[pl.ds(0, slots)], 2)
-    ld_hw = local(hweight.at[0], hw_v, 3)
+    ld_hw = local(hweight.at[0], hw_t, 3)
     ld_1s = local(w1s, w1s_v, 4)
     ld_1n = local(w1n, w1n_v, 5)
     ld_2s = local(w2s, w2s_v, 6)
@@ -224,8 +227,11 @@
             barrier, inc=1, device_id={"node": lax.rem(n + d, nodes)}, device_id_type=MESH_ID
         )
 
-    pairs = coords[0]
-    key = pairs[:, 0:1] * blocks + pairs[:, 1:2]
+    ld_coords.wait()
+    key = coords_v[0:1, :] * blocks + coords_v[1:2, :]
+    t_row = lax.broadcasted_iota(jnp.int32, (slots, slots), 0)
+    t_col = lax.broadcasted_iota(jnp.int32, (slots, slots), 1)
+    key = jnp.sum(jnp.where(t_row == t_col, key, 0), axis=1, keepdims=True)
     slot_id = lax.broadcasted_iota(jnp.int32, (slots, 128), 0)
     pair_id = lax.broadcasted_iota(jnp.int32, (slots, 128), 1)
     named = (key == pair_id) & (slot_id < count[0])
@@ -239,16 +245,18 @@
     scale = 1.0 / math.sqrt(rows * nodes)
     r_id = lax.broadcasted_iota(jnp.int32, (own, own), 0)
     c_id = lax.broadcasted_iota(jnp.int32, (own, own), 1)
-    picked = jnp.where((r_id == c_id) & (flags[...] != 0), 1.0, 0.0).astype(jnp.bfloat16)
+    ld_flags.wait()
+    picked = jnp.where((r_id == c_id) & (flags_v[...] != 0), 1.0, 0.0).astype(jnp.bfloat16)
     ld_up.wait()
     cot[own_rows(f), :] = (nn(picked, up_v[...]) * scale).astype(jnp.bfloat16)
     row_id = lax.broadcasted_iota(jnp.int32, (HALO_ROWS, rows), 0)
     col_id = lax.broadcasted_iota(jnp.int32, (HALO_ROWS, rows), 1)
     parts = []
+    ld_hidx.wait()
     for q in range(nodes):
         want = jnp.full((HALO_ROWS, rows), -1, jnp.int32)
         for k in range(cap):
-            want = jnp.where(row_id == k, hidx[0, q, k], want)
+            want = jnp.where(row_id == k, hidx_s[k, q], want)
         parts.append(jnp.where(want == col_id, 1.0, 0.0).astype(jnp.bfloat16))
     picks = jnp.concatenate(parts, axis=0)
     ld_x.wait()
@@ -286,6 +294,7 @@
         deg[at, :] = 1.0 + nn(tile_rows, ones_a)
 
     ld_hw.wait()
+    hw_v[...] = hw_t[...].T
     ld_1s.wait()
     ld_1n.wait()
     for d, copy in enumerate(halo_copies):
@@ -464,20 +473,8 @@
     for copy in forwards:
         copy.wait_recv()
 
-    for q in range(nodes):
-        at = slice(q * piece, (q + 1) * piece)
-        g1s_o[at, :] = g1fin[q % 2, q // 2, :piece, :].astype(jnp.float32)
-        g1n_o[at, :] = g1fin[q % 2, q // 2, piece:, :].astype(jnp.float32)
-    for k, out in enumerate((g2s_o, g2n_o)):
-        out[...] = jnp.concatenate(
-            [
-                g2fin[g, q % 2, q // 2].astype(jnp.float32)[k * bit:(k + 1) * bit]
-                for g in range(groups)
-                for q in range(nodes)
-            ],
-            axis=0,
-        ).T
-
+    g1_o[...] = g1fin[...]
+    g2_o[...] = g2fin[...]
     for copy in halo_copies + cot_copies + rs_copies + ag_copies + [sib1, sib2]:
         copy.wait_send()
     for batch in z_copies + gathers:
@@ -485,6 +482,39 @@
             copy.wait_send()
     for copy in feat_copies + forwards:
         copy.wait_send()
+
+
+def finish_kernel(
+    groups, nodes, g1, g2, emb, emb_o, g1s_o, g1n_o, g2s_o, g2n_o, v1s, v1n, v2s, v2n, sems
+):
+    piece = g1.shape[2] // 2
+    bit = g2.shape[3] // 2
+    copies = []
+
+    def out(src, dst):
+        copy = pltpu.make_async_copy(src, dst, sems.at[len(copies)])
+        copy.start()
+        copies.append(copy)
+
+    out(emb, emb_o)
+    for k, (val, dst) in enumerate(((v1s, g1s_o), (v1n, g1n_o))):
+        for q in range(nodes):
+            val[q * piece:(q + 1) * piece, :] = g1[
+                q % 2, q // 2, k * piece:(k + 1) * piece, :
+            ].astype(jnp.float32)
+        out(val, dst)
+    for k, (val, dst) in enumerate(((v2s, g2s_o), (v2n, g2n_o))):
+        val[...] = jnp.concatenate(
+            [
+                g2[g, q % 2, q // 2].astype(jnp.float32)[k * bit:(k + 1) * bit]
+                for g in range(groups)
+                for q in range(nodes)
+            ],
+            axis=0,
+        ).T
+        out(val, dst)
+    for copy in copies:
+        copy.wait()
 
 
 def fused_step(
@@ -500,14 +530,18 @@
     piece = 2 * width // nodes
     bit = 2 * outs // groups // nodes
     b16, f32 = jnp.bfloat16, jnp.float32
-    vmem, anywhere, smem = (
-        pl.BlockSpec(memory_space=kind) for kind in (pltpu.VMEM, pl.ANY, pltpu.SMEM)
+    vmem, hbm, smem = (
+        pl.BlockSpec(memory_space=kind) for kind in (pltpu.VMEM, pltpu.HBM, pltpu.SMEM)
     )
     dma = pltpu.SemaphoreType.DMA
     scratch = [
         pltpu.VMEM((rows, width), b16),
         pltpu.VMEM((slots + 1, side, side), b16),
         pltpu.VMEM((slots + 1, side, side), b16),
+        pltpu.VMEM((2, slots), jnp.int32),
+        pltpu.VMEM((1, own), jnp.int32),
+        pltpu.SMEM(halo_index.shape[:0:-1], jnp.int32),
+        pltpu.VMEM((halo, rows), b16),
         pltpu.VMEM((rows, halo), b16),
         pltpu.VMEM((width, units), b16),
         pltpu.VMEM((width, units), b16),
@@ -545,7 +579,7 @@
         pltpu.VMEM((zs, bit, units), b16),
         pltpu.VMEM((zs, bit, units), b16),
         pltpu.VMEM((groups, 2, zs, bit, units), b16),
-        dma((9,)),
+        dma((12,)),
         dma((nodes,)), dma((nodes,)),
         dma((groups,)), dma((groups,)),
         dma((groups,)), dma((groups,)),
@@ -556,8 +590,26 @@
         dma((groups,)), dma((groups,)),
         dma((zs + groups,)), dma((zs + groups,)),
     ]
+    embedding, g1, g2 = pl.pallas_call(
+        functools.partial(step_kernel, groups, nodes),
+        out_shape=(
+            jax.ShapeDtypeStruct((own, outs), b16),
+            jax.ShapeDtypeStruct((2, zs, piece, units), b16),
+            jax.ShapeDtypeStruct((groups, 2, zs, bit, units), b16),
+        ),
+        in_specs=[hbm, hbm, hbm, smem] + [hbm] * 8,
+        out_specs=(vmem,) * 3,
+        scratch_shapes=scratch,
+        compiler_params=pltpu.CompilerParams(
+            collective_id=0, has_side_effects=True, vmem_limit_bytes=56 * 1024 * 1024
+        ),
+    )(
+        features, tile_values, jnp.swapaxes(tile_coords, 1, 2), tile_count,
+        jnp.swapaxes(halo_index, 1, 2), jnp.swapaxes(halo_weight, 1, 2), first_self,
+        first_neighbour, second_self, second_neighbour, upstream, seed_flags.reshape(1, own),
+    )
     return pl.pallas_call(
-        functools.partial(step_kernel, groups, nodes),
+        functools.partial(finish_kernel, groups, nodes),
         out_shape=(
             jax.ShapeDtypeStruct((own, outs), b16),
             jax.ShapeDtypeStruct((width, units), f32),
@@ -565,19 +617,16 @@
             jax.ShapeDtypeStruct((units, outs), f32),
             jax.ShapeDtypeStruct((units, outs), f32),
         ),
-        in_specs=[
-            anywhere, anywhere, vmem, smem, smem, anywhere, anywhere, anywhere, anywhere,
-            anywhere, anywhere, vmem,
+        in_specs=[vmem] * 3,
+        out_specs=(hbm,) * 5,
+        scratch_shapes=[
+            pltpu.VMEM((width, units), f32),
+            pltpu.VMEM((width, units), f32),
+            pltpu.VMEM((units, outs), f32),
+            pltpu.VMEM((units, outs), f32),
+            dma((5,)),
         ],
-        out_specs=(vmem,) * 5,
-        scratch_shapes=scratch,
-        compiler_params=pltpu.CompilerParams(
-            collective_id=0, has_side_effects=True, vmem_limit_bytes=40 * 1024 * 1024
-        ),
-    )(
-        features, tile_values, tile_coords, tile_count, halo_index, halo_weight, first_self,
-        first_neighbour, second_self, second_neighbour, upstream, seed_flags.reshape(1, own),
-    )
+    )(g1, g2, embedding)
 
 
 def solution(mesh):

time: 57.7 us -> 48.6 us (0.84)
  local copies, waits for them, and re-layouts: 10.2 us -> 0 us
  Pallas kernels: 45.7 us -> 47.2 us
    unnamed x28 -> x0, local copies, waits for them, and re-layouts: 10.2 us -> none
    pallas_call x0 -> x1, Pallas kernels: none -> 2.14 us  [fused_step(): pl.pallas_call(functools.partial(finish_kernel, groups, nodes), out_shape...]
    pallas_call x1, Pallas kernels: 45.7 us -> 45 us  [fused_step(): pl.pallas_call(functools.partial(step_kernel, groups, nodes), out_shape=(...]
where the time goes in v2:
time: 48.6 us; the launch traced here: 48.5 us
  Pallas kernels  47.2 us (97%)
  between operations  1.29 us (3%)
    pallas_call x1, Pallas kernels, fused_step(): pl.pallas_call(functools.partial(step_kernel, groups, nodes), out_shape=(...  45 us
    pallas_call x1, Pallas kernels, fused_step(): pl.pallas_call(functools.partial(finish_kernel, groups, nodes), out_shape...  2.14 us

profile of v2, /device:TPU:0, one launch (start us, length us, event | category | flops | bytes accessed | tf_op | source)
XLA Modules:
  0.0 48.5 jit_solution(12684787211885045935)
XLA Ops:
  1.3 45.0 %shard_map.155 = (bf16[256,256]{1,0:T(8,128)(2,1)}, bf16[2,4,64,256]{3,2,1,0:T(8,128)(2,1)}, bf16[4,2,4,16,256]{4,3,2,1,0:T(8,128)(2,1)}) custom-call(bf16[1024,256]{1,0:T(8,128)(2,1)} %feats.1, bf16[1,24,128,128]{3,2,1,0:T(8,128)(2,1)} %tvals.1, s32[1,2,24]{2,1,0:T(2,128)} %bitcast.6, s32[1]{0:T(128)S(6)} %copy.17.count, s32[1,4,8]{2,1,0:T(4,128)} %bitcast.5, ...), custom_call_target="tpu_custom_call" | custom-call | tf_op jit(solution)/shard_map/pallas_call | solution.py:593
  46.3 2.1 %shard_map.156 = (bf16[256,256]{1,0:T(8,128)(2,1)}, f32[256,256]{1,0:T(8,128)}, f32[256,256]{1,0:T(8,128)}, f32[256,256]{1,0:T(8,128)}, f32[256,256]{1,0:T(8,128)}) custom-call(bf16[2,4,64,256]{3,2,1,0:T(8,128)(2,1)} %get-tuple-element.8.g1, bf16[4,2,4,16,256]{4,3,2,1,0:T(8,128)(2,1)} %get-tuple-element.9.g2, bf16[256,256]{1,0:T(8,128)(2,1)} %get-tuple-element.10.emb), custom_call_target="tpu_custom_call" | custom-call | tf_op jit(solution)/shard_map/pallas_call | solution.py:611

commit v3 on v2

--- a/solution.py
+++ b/solution.py
@@ -207,6 +207,14 @@
     def own_rows(p):
         return pl.ds(pl.multiple_of(p * own, own), own)
 
+    barrier = pltpu.get_barrier_semaphore()
+    for d in range(1, groups):
+        pl.semaphore_signal(barrier, inc=1, device_id=feat_id(d), device_id_type=MESH_ID)
+    for d in range(1, nodes):
+        pl.semaphore_signal(
+            barrier, inc=1, device_id={"node": lax.rem(n + d, nodes)}, device_id_type=MESH_ID
+        )
+
     ld_flags = local(flags, flags_v, 9)
     ld_up = local(upstream, up_v, 0)
     ld_hidx = local(hidx.at[0], hidx_s, 10)
@@ -219,14 +227,6 @@
     ld_2s = local(w2s, w2s_v, 6)
     ld_2n = local(w2n, w2n_v, 7)
 
-    barrier = pltpu.get_barrier_semaphore()
-    for d in range(1, groups):
-        pl.semaphore_signal(barrier, inc=1, device_id=feat_id(d), device_id_type=MESH_ID)
-    for d in range(1, nodes):
-        pl.semaphore_signal(
-            barrier, inc=1, device_id={"node": lax.rem(n + d, nodes)}, device_id_type=MESH_ID
-        )
-
     ld_coords.wait()
     key = coords_v[0:1, :] * blocks + coords_v[1:2, :]
     t_row = lax.broadcasted_iota(jnp.int32, (slots, slots), 0)
@@ -249,6 +249,14 @@
     picked = jnp.where((r_id == c_id) & (flags_v[...] != 0), 1.0, 0.0).astype(jnp.bfloat16)
     ld_up.wait()
     cot[own_rows(f), :] = (nn(picked, up_v[...]) * scale).astype(jnp.bfloat16)
+    pl.semaphore_wait(barrier, groups - 1 + nodes - 1)
+    cot_copies = []
+    for d in range(1, groups):
+        mine = cot.at[own_rows(f)]
+        copy = remote(mine, mine, cot_ss.at[d], cot_rs.at[d], feat_id(d))
+        copy.start()
+        cot_copies.append(copy)
+
     row_id = lax.broadcasted_iota(jnp.int32, (HALO_ROWS, rows), 0)
     col_id = lax.broadcasted_iota(jnp.int32, (HALO_ROWS, rows), 1)
     parts = []
@@ -263,20 +271,12 @@
     hsend[...] = nn(picks, x_v[...]).astype(jnp.bfloat16).reshape(hsend.shape)
     hrecv[n] = hsend[n]
 
-    pl.semaphore_wait(barrier, groups - 1 + nodes - 1)
     halo_copies = []
     for d in range(1, nodes):
         q = lax.rem(n + d, nodes)
         copy = remote(hsend.at[q], hrecv.at[n], halo_ss.at[d], halo_rs.at[d], {"node": q})
         copy.start()
         halo_copies.append(copy)
-    cot_copies = []
-    for d in range(1, groups):
-        mine = cot.at[own_rows(f)]
-        copy = remote(mine, mine, cot_ss.at[d], cot_rs.at[d], feat_id(d))
-        copy.start()
-        cot_copies.append(copy)
-
     ld_t.wait()
     ld_slot.wait()
     for r in range(blocks):
@@ -324,10 +324,6 @@
         rs_copies.append(copy)
     total = first_layer(f)
 
-    for k in range(groups):
-        at = slice(k * own, (k + 1) * own)
-        x_t[:, at] = x_v[at, :].T
-        agg_t[:, at] = agg[at, :].T
     for copy in rs_copies:
         copy.wait_recv()
     for d in range(1, groups):
@@ -339,6 +335,11 @@
         copy = remote(mine, mine, ag_ss.at[d], ag_rs.at[d], feat_id(d))
         copy.start()
         ag_copies.append(copy)
+
+    for k in range(groups):
+        at = slice(k * own, (k + 1) * own)
+        x_t[:, at] = x_v[at, :].T
+        agg_t[:, at] = agg[at, :].T
 
     for t in range(slots):
         tiles_t[t] = tiles[t].T
@@ -408,9 +409,10 @@
     sib2 = remote(s2.at[1 - c], r2s, sib_ss.at[1], sib_rs.at[1], sib_id)
     sib2.start()
 
-    z_copies = []
-    for i, (sib, mine, theirs, comb, dest) in enumerate(
-        ((sib1, s1, r1s, comb1, r1z), (sib2, s2, r2s, comb2, r2z))
+    z_copies = [None, None]
+    for i, sib, mine, theirs, comb, dest in (
+        (1, sib2, s2, r2s, comb2, r2z),
+        (0, sib1, s1, r1s, comb1, r1z),
     ):
         sib.wait_recv()
         comb[...] = (mine[c].astype(jnp.float32) + theirs[...].astype(jnp.float32)).astype(
@@ -423,14 +425,15 @@
             )
             copy.start()
             batch.append(copy)
-        z_copies.append(batch)
+        z_copies[i] = batch
 
     at = own_rows(f)
     emb_o[...] = (nn(hid[at, :], w2s_v[...]) + nn(mean[at, :], w2n_v[...])).astype(jnp.bfloat16)
 
-    gathers = []
-    for i, (comb, dest, final) in enumerate(
-        ((comb1, r1z, g1fin.at[c]), (comb2, r2z, g2fin.at[f, c]))
+    gathers = [None, None]
+    for i, comb, dest, final in (
+        (1, comb2, r2z, g2fin.at[f, c]),
+        (0, comb1, r1z, g1fin.at[c]),
     ):
         total = comb[z].astype(jnp.float32)
         for d in range(1, zs):
@@ -447,7 +450,7 @@
             )
             copy.start()
             batch.append(copy)
-        gathers.append(batch)
+        gathers[i] = batch
 
     def forward(ref, i):
         copy = remote(ref, ref, fw_ss.at[i], fw_rs.at[i], sib_id)

time: 48.6 us -> 46.3 us (0.953)
  Pallas kernels: 47.2 us -> 44.8 us
    pallas_call x1, Pallas kernels: 45 us -> 42.7 us  [fused_step(): pl.pallas_call(functools.partial(step_kernel, groups, nodes), out_shape=(...]
where the time goes in v3:
time: 46.3 us; the launch traced here: 46.1 us
  Pallas kernels  44.8 us (97%)
  between operations  1.29 us (3%)
    pallas_call x1, Pallas kernels, fused_step(): pl.pallas_call(functools.partial(step_kernel, groups, nodes), out_shape=(...  42.7 us
    pallas_call x1, Pallas kernels, fused_step(): pl.pallas_call(functools.partial(finish_kernel, groups, nodes), out_shape...  2.14 us

profile of v3, /device:TPU:0, one launch (start us, length us, event | category | flops | bytes accessed | tf_op | source)
XLA Modules:
  0.0 46.1 jit_solution(5346196116607994744)
XLA Ops:
  1.3 42.7 %shard_map.155 = (bf16[256,256]{1,0:T(8,128)(2,1)}, bf16[2,4,64,256]{3,2,1,0:T(8,128)(2,1)}, bf16[4,2,4,16,256]{4,3,2,1,0:T(8,128)(2,1)}) custom-call(bf16[1024,256]{1,0:T(8,128)(2,1)} %feats.1, bf16[1,24,128,128]{3,2,1,0:T(8,128)(2,1)} %tvals.1, s32[1,2,24]{2,1,0:T(2,128)} %bitcast.6, s32[1]{0:T(128)S(6)} %copy.17.count, s32[1,4,8]{2,1,0:T(4,128)} %bitcast.5, ...), custom_call_target="tpu_custom_call" | custom-call | tf_op jit(solution)/shard_map/pallas_call | solution.py:596
  44.0 2.1 %shard_map.156 = (bf16[256,256]{1,0:T(8,128)(2,1)}, f32[256,256]{1,0:T(8,128)}, f32[256,256]{1,0:T(8,128)}, f32[256,256]{1,0:T(8,128)}, f32[256,256]{1,0:T(8,128)}) custom-call(bf16[2,4,64,256]{3,2,1,0:T(8,128)(2,1)} %get-tuple-element.8.g1, bf16[4,2,4,16,256]{4,3,2,1,0:T(8,128)(2,1)} %get-tuple-element.9.g2, bf16[256,256]{1,0:T(8,128)(2,1)} %get-tuple-element.10.emb), custom_call_target="tpu_custom_call" | custom-call | tf_op jit(solution)/shard_map/pallas_call | solution.py:614

commit v4 on v3

--- a/solution.py
+++ b/solution.py
@@ -202,6 +202,34 @@
     def z_id(d):
         return {"node": z_at(d) * 2 + c}
 
+    feat_a = f + 1 - 2 * lax.rem(f, 2)
+    feat_b = lax.rem(f + 2, groups)
+    feat_c = lax.rem(feat_a + 2, groups)
+
+    def half(ref, p, k):
+        size = own // 2
+        return ref.at[pl.ds(pl.multiple_of(p * own + k * size, size), size)]
+
+    def gather_copy(ref, ss, rs, i, p, k, target):
+        piece = half(ref, p, k)
+        copy = remote(piece, piece, ss.at[i], rs.at[i], {"feat": target})
+        copy.start()
+        return copy
+
+    def gather_start(ref, ss, rs):
+        return [
+            gather_copy(ref, ss, rs, i, f, k, target)
+            for i, (k, target) in enumerate(
+                ((0, feat_a), (1, feat_b), (1, feat_a), (0, feat_b))
+            )
+        ]
+
+    def gather_forward(ref, ss, rs, copies):
+        copies[0].wait_recv()
+        copies.append(gather_copy(ref, ss, rs, 4, feat_a, 0, feat_b))
+        copies[1].wait_recv()
+        copies.append(gather_copy(ref, ss, rs, 5, feat_b, 1, feat_a))
+
     sib_id = {"node": z * 2 + (1 - c)}
 
     def own_rows(p):
@@ -250,12 +278,7 @@
     ld_up.wait()
     cot[own_rows(f), :] = (nn(picked, up_v[...]) * scale).astype(jnp.bfloat16)
     pl.semaphore_wait(barrier, groups - 1 + nodes - 1)
-    cot_copies = []
-    for d in range(1, groups):
-        mine = cot.at[own_rows(f)]
-        copy = remote(mine, mine, cot_ss.at[d], cot_rs.at[d], feat_id(d))
-        copy.start()
-        cot_copies.append(copy)
+    cot_copies = gather_start(cot, cot_ss, cot_rs)
 
     row_id = lax.broadcasted_iota(jnp.int32, (HALO_ROWS, rows), 0)
     col_id = lax.broadcasted_iota(jnp.int32, (HALO_ROWS, rows), 1)
@@ -293,6 +316,7 @@
         numer[at, :] = nn(tile_rows, x_v[...])
         deg[at, :] = 1.0 + nn(tile_rows, ones_a)
 
+    gather_forward(cot, cot_ss, cot_rs, cot_copies)
     ld_hw.wait()
     hw_v[...] = hw_t[...].T
     ld_1s.wait()
@@ -329,16 +353,14 @@
     for d in range(1, groups):
         total = total + precv[d].astype(jnp.float32)
     pre[own_rows(f), :] = total.astype(jnp.bfloat16)
-    ag_copies = []
-    for d in range(1, groups):
-        mine = pre.at[own_rows(f)]
-        copy = remote(mine, mine, ag_ss.at[d], ag_rs.at[d], feat_id(d))
-        copy.start()
-        ag_copies.append(copy)
+    ag_copies = gather_start(pre, ag_ss, ag_rs)
 
     for k in range(groups):
         at = slice(k * own, (k + 1) * own)
         x_t[:, at] = x_v[at, :].T
+    gather_forward(pre, ag_ss, ag_rs, ag_copies)
+    for k in range(groups):
+        at = slice(k * own, (k + 1) * own)
         agg_t[:, at] = agg[at, :].T
 
     for t in range(slots):
@@ -350,7 +372,7 @@
             ]
     ld_2s.wait()
     ld_2n.wait()
-    for copy in cot_copies:
+    for copy in cot_copies[2:]:
         copy.wait_recv()
     for k in range(groups):
         at = slice(k * own, (k + 1) * own)
@@ -378,9 +400,10 @@
         gpre[at, :] = (grad_h[at, :] * slope).astype(jnp.bfloat16)
 
     activate(f)
-    for d in range(groups - 1, 0, -1):
-        ag_copies[d - 1].wait_recv()
-        activate(feat_at(groups - d))
+    for arrived, p in (((2,), feat_a), ((3,), feat_b), ((4, 5), feat_c)):
+        for i in arrived:
+            ag_copies[i].wait_recv()
+        activate(p)
 
     piece = width // nodes
     for k, lhs in enumerate((x_t, agg_t)):
@@ -584,9 +607,9 @@
         pltpu.VMEM((groups, 2, zs, bit, units), b16),
         dma((12,)),
         dma((nodes,)), dma((nodes,)),
+        dma((6,)), dma((6,)),
         dma((groups,)), dma((groups,)),
-        dma((groups,)), dma((groups,)),
-        dma((groups,)), dma((groups,)),
+        dma((6,)), dma((6,)),
         dma((2,)), dma((2,)),
         dma((2, zs)), dma((2, zs)),
         dma((2, zs)), dma((2, zs)),
@@ -634,7 +657,7 @@
 
 def solution(mesh):
     groups, nodes = mesh.shape["feat"], mesh.shape["node"]
-    step = functools.partial(fused_step, groups, nodes) if nodes <= FUSED_NODES else on_device
+    step = functools.partial(fused_step, groups, nodes) if (groups, nodes) == (4, FUSED_NODES) else on_device
     in_specs = (
         P("node", "feat"),
         P("node", None, None, None),

time: 46.3 us -> 45.4 us (0.981)
  Pallas kernels: 44.8 us -> 43.9 us
    pallas_call x1, Pallas kernels: 42.7 us -> 41.8 us  [fused_step(): pl.pallas_call(functools.partial(step_kernel, groups, nodes), out_shape=(...]
where the time goes in v4:
time: 45.4 us; the launch traced here: 45.2 us
  Pallas kernels  43.9 us (97%)
  between operations  1.29 us (3%)
    pallas_call x1, Pallas kernels, fused_step(): pl.pallas_call(functools.partial(step_kernel, groups, nodes), out_shape=(...  41.8 us
    pallas_call x1, Pallas kernels, fused_step(): pl.pallas_call(functools.partial(finish_kernel, groups, nodes), out_shape...  2.14 us

profile of v4, /device:TPU:0, one launch (start us, length us, event | category | flops | bytes accessed | tf_op | source)
XLA Modules:
  0.0 45.2 jit_solution(1372927211926362423)
XLA Ops:
  1.3 41.8 %shard_map.155 = (bf16[256,256]{1,0:T(8,128)(2,1)}, bf16[2,4,64,256]{3,2,1,0:T(8,128)(2,1)}, bf16[4,2,4,16,256]{4,3,2,1,0:T(8,128)(2,1)}) custom-call(bf16[1024,256]{1,0:T(8,128)(2,1)} %feats.1, bf16[1,24,128,128]{3,2,1,0:T(8,128)(2,1)} %tvals.1, s32[1,2,24]{2,1,0:T(2,128)} %bitcast.6, s32[1]{0:T(128)S(6)} %copy.17.count, s32[1,4,8]{2,1,0:T(4,128)} %bitcast.5, ...), custom_call_target="tpu_custom_call" | custom-call | tf_op jit(solution)/shard_map/pallas_call | solution.py:619
  43.1 2.1 %shard_map.156 = (bf16[256,256]{1,0:T(8,128)(2,1)}, f32[256,256]{1,0:T(8,128)}, f32[256,256]{1,0:T(8,128)}, f32[256,256]{1,0:T(8,128)}, f32[256,256]{1,0:T(8,128)}) custom-call(bf16[2,4,64,256]{3,2,1,0:T(8,128)(2,1)} %get-tuple-element.8.g1, bf16[4,2,4,16,256]{4,3,2,1,0:T(8,128)(2,1)} %get-tuple-element.9.g2, bf16[256,256]{1,0:T(8,128)(2,1)} %get-tuple-element.10.emb), custom_call_target="tpu_custom_call" | custom-call | tf_op jit(solution)/shard_map/pallas_call | solution.py:637
